TPU v7x, 32 devices: a whole 2x2x4 slice. The times are simulated.
32 devices in a mesh: rep: 2 (over y), ep: 4 (over z), tr: 2 (over x), tc: 2 (over core).
Axes of the slice: x: 2, y: 2, z: 4, core: 2. Of those that a mesh axis runs over, the one named last changes fastest.
Arguments:
- residual: bfloat16 [2048, 6144], P(('rep', 'ep', 'tc'), 'tr'), parts along dimension 0, may hold values from -24 to 24
- query_rows: bfloat16 [2048, 6144], P(('rep', 'ep', 'tc'), 'tr'), parts along dimension 0, may hold values from -4.5 to 4.5
- key_rows: bfloat16 [2048, 1024], P(('rep', 'ep', 'tc'), 'tr'), parts along dimension 0, may hold values from -10 to 10
- value_rows: bfloat16 [2048, 1024], P(('rep', 'ep', 'tc'), 'tr'), parts along dimension 0, may hold values from -6 to 6
- segments: int32 [2048], P('rep'), parts along dimension 0, may hold values from 0 to 7, never falling along the last dimension, each value on 1 to 512 neighbouring positions
- routes: int32 [2048, 2], P(('rep', 'ep', 'tc')), parts along dimension 0, may hold values from 0 to 7, as said below
- gate_weights: float32 [2048, 2], P(('rep', 'ep', 'tc')), parts along dimension 0, may hold values from 0.3 to 1
- norm_gain: float32 [6144], P('tr'), may hold values from 0.1 to 1.9
- w_gate: bfloat16 [6144, 16384], P('tr', ('ep', 'tc')), may hold values from -0.078125 to 0.078125
- w_up: bfloat16 [6144, 16384], P('tr', ('ep', 'tc')), may hold values from -0.078125 to 0.078125
- w_down: bfloat16 [16384, 6144], P(('ep', 'tc'), 'tr'), may hold values from -0.0625 to 0.0625
Outputs:
- attention: bfloat16 [2048, 6144], P(('rep', 'ep', 'tc'), 'tr'), parts along dimension 0
- expert_mix: bfloat16 [2048, 6144], P(('rep', 'ep', 'tc'), 'tr'), parts along dimension 0
There are 2 independent parts, one for each index of `rep`. A program takes and returns all parts, laid end to end along the dimension named above; an argument that names none is the same for every part. Nothing has to cross between parts.
Inputs may be any that keep to these rules, and one draw needn't show every extreme that they name: `routes`: each row names two different experts. The rows of one device (an aligned block of 128 rows) name each expert below 2 at most 32 times, and in every draw one expert below 2 is named exactly 32 times by the rows of every device.
All inputs are finite; a program needn't handle non-finite values.
Results may differ from a plain program's by a relative error of at most 0.024.
Values may be sent and summed in bfloat16 or wider, within the bound.
A program may use at most 128 MiB of HBM per device.

v0:
```python
import math

import jax
import jax.numpy as jnp
from jax import lax
from jax.sharding import PartitionSpec as P

D = 6144
QH = 48
KVH = 8
HD = 128
EXPW = 2


masked_score = -1e30
key_block = 512


def score_block(
    running, key_piece, value_piece, offset, query_heads, row_pos, row_seg, segments, score_scale
):
    best_score, denominator, accumulated = running
    length = key_piece.shape[0]
    head_count = query_heads.shape[0]
    key_heads = key_piece.reshape(length, head_count, HD)
    value_heads = value_piece.reshape(length, head_count, HD)
    key_pos = offset + jnp.arange(length, dtype=jnp.int32)
    key_seg = lax.dynamic_slice_in_dim(segments, offset, length)
    visible = (key_pos[None, :] <= row_pos[:, None]) & (key_seg[None, :] == row_seg[:, None])
    scores = (
        jnp.einsum("hrd,khd->hrk", query_heads, key_heads, preferred_element_type=jnp.float32)
        * score_scale
    )
    scores = jnp.where(visible[None], scores, masked_score)
    new_best = jnp.maximum(best_score, jnp.max(scores, axis=2))
    exponent = jnp.where(visible[None], jnp.exp(scores - new_best[:, :, None]), 0.0)
    factor = jnp.exp(best_score - new_best)
    denominator = denominator * factor + jnp.sum(exponent, axis=2)
    accumulated = accumulated * factor[:, :, None] + jnp.einsum(
        "hrk,khd->hrd",
        exponent.astype(jnp.bfloat16),
        value_heads,
        preferred_element_type=jnp.float32,
    )
    return (new_best, denominator, accumulated)


def fold_context(running, pieces, start, query_heads, row_pos, row_seg, segments, score_scale):
    key_piece, value_piece = pieces
    total_rows = key_piece.shape[0]
    for offset_rows in range(0, total_rows, key_block):
        width_rows = min(key_block, total_rows - offset_rows)
        running = score_block(
            running,
            key_piece[offset_rows : offset_rows + width_rows],
            value_piece[offset_rows : offset_rows + width_rows],
            start + offset_rows,
            query_heads,
            row_pos,
            row_seg,
            segments,
            score_scale,
        )
    return running


def shards(
    residual,
    query_rows,
    key_rows,
    value_rows,
    segments,
    routes,
    gate_weights,
    norm_gain,
    w_gate,
    w_up,
    w_down,
):
    tokens = residual.shape[0]
    feature_width = residual.shape[1]
    kv_count = key_rows.shape[1] // HD
    group_size = QH // KVH
    row_count = tokens * group_size
    first_token = lax.axis_index(("ep", "tc")) * tokens
    token_pos = first_token + jnp.arange(tokens, dtype=jnp.int32)
    token_seg = lax.dynamic_slice_in_dim(segments, first_token, tokens)
    row_pos = jnp.repeat(token_pos, group_size)
    row_seg = jnp.repeat(token_seg, group_size)
    query_heads = (
        query_rows.reshape(tokens, kv_count, group_size, HD)
        .transpose(1, 0, 2, 3)
        .reshape(kv_count, row_count, HD)
    )
    score_scale = 1.0 / math.sqrt(HD)
    initial = (
        jnp.full((kv_count, row_count), masked_score, jnp.float32),
        jnp.zeros((kv_count, row_count), jnp.float32),
        jnp.zeros((kv_count, row_count, HD), jnp.float32),
    )
    folded = fold_context(
        initial,
        (
            lax.all_gather(key_rows, ("ep", "tc"), axis=0, tiled=True),
            lax.all_gather(value_rows, ("ep", "tc"), axis=0, tiled=True),
        ),
        jnp.int32(0),
        query_heads,
        row_pos,
        row_seg,
        segments,
        score_scale,
    )
    heads_out = folded[2] / folded[1][:, :, None]
    attention = (
        heads_out.reshape(kv_count, tokens, group_size, HD)
        .transpose(1, 0, 2, 3)
        .reshape(tokens, feature_width)
        .astype(jnp.bfloat16)
    )
    mixed_rows = (residual.astype(jnp.float32) + attention.astype(jnp.float32)).astype(jnp.bfloat16)
    mixed_wide = mixed_rows.astype(jnp.float32)
    squares = lax.psum(jnp.sum(mixed_wide * mixed_wide, axis=1), "tr")
    inv_rms = lax.rsqrt(squares / D + 1e-05)
    normed = (mixed_wide * inv_rms[:, None] * norm_gain[None, :]).astype(jnp.bfloat16)
    capacity = tokens // 4
    expert_ids = jnp.arange(EXPW, dtype=jnp.int32)
    matches = routes[:, None, :] == expert_ids[None, :, None]
    chosen = jnp.any(matches, axis=2)
    weight_cols = jnp.sum(jnp.where(matches, gate_weights[:, None, :], 0.0), axis=2)
    slot_index = jnp.cumsum(chosen.astype(jnp.int32), axis=0) - 1
    slot_ids = jnp.arange(capacity, dtype=jnp.int32)
    placement_table = (slot_index.T[:, None, :] == slot_ids[None, :, None]) & chosen.T[:, None, :]
    packed = jnp.einsum(
        "ect,td->ecd",
        placement_table.astype(jnp.bfloat16),
        normed,
        preferred_element_type=jnp.float32,
    ).astype(jnp.bfloat16)
    ep_count = lax.axis_size("ep")
    tc_count = lax.axis_size("tc")
    share_count = ep_count // EXPW
    spread = jnp.repeat(packed, share_count, axis=0)
    outgoing = jnp.broadcast_to(
        spread[:, None], (ep_count, tc_count, capacity, feature_width)
    ).reshape(ep_count * tc_count, capacity, feature_width)
    arrived = lax.all_to_all(outgoing, ("ep", "tc"), split_axis=0, concat_axis=0, tiled=True)
    slot_rows = arrived.reshape(ep_count * tc_count * capacity, feature_width)
    part_gate = jnp.dot(slot_rows, w_gate, preferred_element_type=jnp.float32)
    part_up = jnp.dot(slot_rows, w_up, preferred_element_type=jnp.float32)
    gate_sum, up_sum = (
        lax.psum(part_gate.astype(jnp.bfloat16), "tr").astype(jnp.float32),
        lax.psum(part_up.astype(jnp.bfloat16), "tr").astype(jnp.float32),
    )
    hidden = (jax.nn.silu(gate_sum) * up_sum).astype(jnp.bfloat16)
    down_part = (
        jnp.dot(hidden, w_down, preferred_element_type=jnp.float32)
        .astype(jnp.bfloat16)
        .reshape(ep_count * tc_count, capacity, feature_width)
    )
    returned = lax.all_to_all(down_part, ("ep", "tc"), split_axis=0, concat_axis=0, tiled=True)
    per_expert = jnp.sum(
        returned.astype(jnp.float32).reshape(EXPW, share_count * tc_count, capacity, feature_width),
        axis=1,
    )
    combine_table = placement_table.astype(jnp.float32) * weight_cols.T[:, None, :]
    expert_mix = jnp.einsum(
        "ect,ecd->td", combine_table, per_expert, precision=lax.Precision.HIGHEST
    ).astype(jnp.bfloat16)
    return (attention, expert_mix)


def solution(mesh):
    in_specs = (
        P(("rep", "ep", "tc"), "tr"),
        P(("rep", "ep", "tc"), "tr"),
        P(("rep", "ep", "tc"), "tr"),
        P(("rep", "ep", "tc"), "tr"),
        P("rep"),
        P(("rep", "ep", "tc"), None),
        P(("rep", "ep", "tc"), None),
        P("tr"),
        P("tr", ("ep", "tc")),
        P("tr", ("ep", "tc")),
        P(("ep", "tc"), "tr"),
    )
    out_specs = (P(("rep", "ep", "tc"), "tr"), P(("rep", "ep", "tc"), "tr"))
    return jax.shard_map(shards, mesh=mesh, in_specs=in_specs, out_specs=out_specs, check_vma=False)
```

profile of v0, /device:TPU:0, one launch (start us, length us, event | category | flops | bytes accessed | tf_op | source)
XLA Modules:
  0.0 260.3 jit_solution(10851738905835051925)
XLA Ops:
  7.2 1.7 copy.44
  9.0 1.7 copy.47
  10.8 0.8 dynamic_slice.10
  12.0 1.5 copy.42
  13.5 0.7 copy.43
  14.2 0.4 copy.58
  15.0 0.7 fusion.21
  15.7 21.2 %all-gather.3.cloned.1.call-done = bf16[1024,512]{0,1:T(8,128)(2,1)} async-done(((bf16[128,512]{0,1:T(8,128)(2,1)}), bf16[1024,512]{0,1:T(8,128)(2,1)}) %all-gather.3.cloned.1.call-update) | async-done | bytes 1048592 | tf_op jit(solution)/shard_map/all_gather | solution.py:104
  36.9 1.3 fusion.55
  38.2 4.0 %fusion = (f32[4,768]{1,0:T(4,128)S(1)}, f32[4,768,512]{1,2,0:T(8,128)}) fusion(pred[768,512]{0,1:T(8,128)(4,1)S(1)} %get-tuple-element.17, bf16[512,4,128]{0,2,1:T(8,128)(2,1)S(1)} %bitcast.52, bf16[4,768,128]{2,0,1:T(4,128)(2,1)S(1)} %bitcast.43), kind=kOutput, calls=%fused_computation.4 | convolution fusion | flops 407368704 | bytes 8007680 | tf_op jit(solution)/shard_map/hrd,khd->hrk/dot_general | solution.py:31
  42.2 4.0 %fusion.1 = (f32[4,768]{1,0:T(4,128)S(1)}, f32[4,768,512]{1,2,0:T(8,128)}) fusion(pred[768,512]{0,1:T(8,128)(4,1)S(1)} %get-tuple-element.18, bf16[512,4,128]{0,2,1:T(8,128)(2,1)S(1)} %bitcast.51, bf16[4,768,128]{2,0,1:T(4,128)(2,1)S(1)} %bitcast.44), kind=kOutput, calls=%fused_computation.5 | convolution fusion | flops 407368704 | bytes 8007680 | tf_op jit(solution)/shard_map/hrd,khd->hrk/dot_general | solution.py:31
  46.2 15.5 %all-gather.5.cloned.1.call-done = bf16[1024,512]{0,1:T(8,128)(2,1)} async-done(((bf16[128,512]{0,1:T(8,128)(2,1)}), bf16[1024,512]{0,1:T(8,128)(2,1)}) %all-gather.5.cloned.1.call-update) | async-done | bytes 1048592 | tf_op jit(solution)/shard_map/all_gather | solution.py:105
  61.7 1.3 fusion.54
  63.0 5.2 %fusion.7 = f32[4,768,128]{2,1,0:T(8,128)S(1)} fusion(bf16[512,4,128]{0,2,1:T(8,128)(2,1)S(1)} %bitcast.57, f32[4,768,512]{1,2,0:T(8,128)} %get-tuple-element.24, f32[4,768]{1,0:T(4,128)S(1)} %get-tuple-element.15, pred[768,512]{0,1:T(8,128)(4,1)S(1)} %get-tuple-element.18), kind=kOutput, calls=%fused_computation.15 | convolution fusion | flops 410517504 | bytes 8794112 | tf_op jit(solution)/shard_map/hrk,khd->hrd/dot_general | solution.py:39
  68.2 1.2 copy-done
  69.4 3.1 %fusion.2 = (f32[4,768]{1,0:T(4,128)S(1)}, f32[4,768]{1,0:T(4,128)S(1)}) fusion(f32[4,768,512]{1,2,0:T(8,128)S(1)} %bitcast.42, f32[4,768]{1,0:T(4,128)S(1)} %get-tuple-element.16, pred[768,512]{0,1:T(8,128)(4,1)S(1)} %get-tuple-element.17, f32[4,768]{1,0:T(4,128)S(1)} %get-tuple-element.15, f32[4,768,512]{1,2,0:T(8,128)S(1)} %copy-done, ...), kind=kLoop, calls=%fused_computation.6 | loop fusion | flops 15722496 | bytes 13418496 | tf_op jit(solution)/shard_map/reduce_sum | solution.py:38
  72.6 3.5 %divide_convert_fusion = bf16[4,768,128]{2,1,0:T(8,128)(2,1)S(1)} fusion(f32[4,768,128]{2,1,0:T(8,128)S(1)} %fusion.7, bf16[512,4,128]{0,2,1:T(8,128)(2,1)S(1)} %bitcast.56, f32[4,768,512]{1,2,0:T(8,128)S(1)} %bitcast.42, f32[4,768]{1,0:T(4,128)S(1)} %get-tuple-element.16, pred[768,512]{0,1:T(8,128)(4,1)S(1)} %get-tuple-element.17, ...), kind=kOutput, calls=%fused_computation.34 | convolution fusion | flops 412483584 | bytes 9617408 | tf_op jit(solution)/shard_map/hrk,khd->hrd/dot_general | solution.py:39
  76.1 0.6 copy.54
  76.8 0.8 copy.55
  77.5 0.5 fusion.18
  78.0 5.1 %psum.21 = f32[128]{0:T(128)S(1)} all-reduce(f32[128]{0:T(128)S(1)} %fusion.18), channel_id=1, replica_groups=mesh['rep'=2,'ep'=4,'tr'=2,'tc'=2] {'tr'}, use_global_device_ids=true, to_apply=%region_8.9 | all-reduce | flops 128 | bytes 1024 | tf_op jit(solution)/shard_map/psum | solution.py:123
  83.1 0.7 convolution_convert_fusion.1
  84.1 41.6 %all_to_all.10 = bf16[8,32,3072]{2,1,0:T(8,128)(2,1)S(1)} all-to-all(bf16[8,32,3072]{2,1,0:T(8,128)(2,1)S(1)} %bitcast.47), channel_id=1, replica_groups=mesh['rep'=2,'ep'=4,'tr'=2,'tc'=2] {'ep','tc'}, dimensions={0} | all-to-all | bytes 3145728 | tf_op jit(solution)/shard_map/all_to_all | solution.py:147
  125.7 7.7 %convolution_convert_fusion.2 = bf16[256,2048]{1,0:T(8,128)(2,1)} fusion(bf16[256,3072]{1,0:T(8,128)(2,1)S(1)} %bitcast.54, bf16[3072,2048]{1,0:T(8,128)(2,1)} %param.20), kind=kOutput, calls=%fused_computation.21 | convolution fusion | flops 3221749760 | bytes 15204352 | tf_op jit(solution)/shard_map/dot_general | solution.py:150
  133.4 4.5 %convolution_convert_fusion.3 = bf16[256,2048]{1,0:T(8,128)(2,1)} fusion(bf16[256,3072]{1,0:T(8,128)(2,1)S(1)} %bitcast.55, bf16[3072,2048]{1,0:T(8,128)(2,1)S(1)} %bitcast.62), kind=kOutput, calls=%fused_computation.22 | convolution fusion | flops 3221749760 | bytes 15204352 | tf_op jit(solution)/shard_map/dot_general | solution.py:149
  137.9 60.7 %all-reduce.3.cloned.1.call-done = (bf16[256,2048]{1,0:T(8,128)(2,1)}, bf16[256,2048]{1,0:T(8,128)(2,1)}) async-done(((bf16[256,2048]{1,0:T(8,128)(2,1)}, bf16[256,2048]{1,0:T(8,128)(2,1)}), (bf16[256,2048]{1,0:T(8,128)(2,1)}, bf16[256,2048]{1,0:T(8,128)(2,1)})) %all-reduce.3.cloned.1.call-update) | async-done | bytes 2097168 | tf_op jit(solution)/shard_map/psum | solution.py:153
  198.6 10.0 %convolution_convert_fusion = bf16[256,3072]{1,0:T(8,128)(2,1)} fusion(bf16[2048,3072]{1,0:T(8,128)(2,1)} %param.21, bf16[256,2048]{1,0:T(8,128)(2,1)} %get-tuple-element.6, bf16[256,2048]{1,0:T(8,128)(2,1)} %get-tuple-element.7), kind=kOutput, calls=%fused_computation.10 | convolution fusion | flops 3226206208 | bytes 16252928 | tf_op jit(solution)/shard_map/dot_general | solution.py:157
  208.6 4.7 %all-to-all-start.1 = ((bf16[8,32,3072]{2,1,0:T(8,128)(2,1)}), bf16[8,32,3072]{2,1,0:T(8,128)(2,1)S(1)}, u32[]{:S(2)}, u32[]{:S(2)}) async-start(bf16[8,32,3072]{2,1,0:T(8,128)(2,1)} %bitcast.53), calls=%async_computation.1 | async-start | bytes 3145728 | tf_op jit(solution)/shard_map/all_to_all | solution.py:161
  213.4 1.2 copy.60
  214.6 36.6 %all-to-all-done.1 = bf16[8,32,3072]{2,1,0:T(8,128)(2,1)S(1)} async-done(((bf16[8,32,3072]{2,1,0:T(8,128)(2,1)}), bf16[8,32,3072]{2,1,0:T(8,128)(2,1)S(1)}, u32[]{:S(2)}, u32[]{:S(2)}) %all-to-all-start.1) | async-done | bytes 1572896 | tf_op jit(solution)/shard_map/all_to_all | solution.py:161
  251.2 0.2 convert_reduce_fusion
  251.4 2.3 fusion.6
  (48 shorter events, 1.4 us)
Async XLA Ops:
  7.2 7.8 %copy-start.2 = (s32[1024]{0:T(1024)S(1)}, s32[1024]{0:T(1024)}, u32[]{:S(2)}) copy-start(s32[1024]{0:T(1024)} %param.15) | copy-start | bytes 12292
  7.2 7.0 %copy-start.1 = (bf16[128,3072]{1,0:T(8,128)(2,1)S(1)}, bf16[128,3072]{1,0:T(8,128)(2,1)}, u32[]{:S(2)}) copy-start(bf16[128,3072]{1,0:T(8,128)(2,1)} %param.11) | copy-start | bytes 2359300
  7.2 7.4 %copy-start.3 = (s32[128,2]{0,1:T(2,128)S(1)}, s32[128,2]{0,1:T(2,128)}, u32[]{:S(2)}) copy-start(s32[128,2]{0,1:T(2,128)} %param.16) | copy-start | bytes 3076
  7.2 29.7 %all-gather.3.cloned.1.call-start = ((), (), s32[]{:S(2)}) async-start(), calls=%async_computation.2 | async-start | bytes 1179648 | tf_op jit(solution)/shard_map/all_gather | solution.py:104
  9.0 52.7 %all-gather.5.cloned.1.call-start = ((), (), s32[]{:S(2)}) async-start(), calls=%async_computation.3 | async-start | bytes 1179648 | tf_op jit(solution)/shard_map/all_gather | solution.py:105
  10.7 187.9 %all-reduce.3.cloned.1.call-start = ((), (), s32[]{:S(2)}) async-start(), calls=%async_computation.4 | async-start | bytes 4194304 | tf_op jit(solution)/shard_map/psum | solution.py:153
  62.9 5.2 %slice-start = ((s8[6291456]{0:T(1024)(128)(4,1)}), s8[4194304]{0:T(1024)(128)(4,1)S(1)}, s32[]{:S(2)}) async-start(s8[6291456]{0:T(1024)(128)(4,1)} %bitcast.41), calls=%async_computation.5 | async-start | bytes 8388608
  63.0 5.2 %slice-start.1 = ((s8[6291456]{0:T(1024)(128)(4,1)}), s8[2097152]{0:T(1024)(128)(4,1)S(1)}, s32[]{:S(2)}) async-start(s8[6291456]{0:T(1024)(128)(4,1)} %bitcast.41), calls=%async_computation.6 | async-start | bytes 4194304
  63.0 6.5 %copy-start = (f32[4,768,512]{1,2,0:T(8,128)S(1)}, f32[4,768,512]{1,2,0:T(8,128)}, u32[]{:S(2)}) copy-start(f32[4,768,512]{1,2,0:T(8,128)} %get-tuple-element.24) | copy-start | bytes 18874372
  76.1 7.0 %copy-start.5 = (f32[3072]{0:T(1024)S(1)}, f32[3072]{0:T(1024)}, u32[]{:S(2)}) copy-start(f32[3072]{0:T(1024)} %param.18) | copy-start | bytes 36868
  84.1 49.3 %slice-start.2 = ((s8[12582912]{0:T(1024)(128)(4,1)}), s8[4194304]{0:T(1024)(128)(4,1)S(1)}, s32[]{:S(2)}) async-start(s8[12582912]{0:T(1024)(128)(4,1)} %bitcast.61), calls=%async_computation.7 | async-start | bytes 8388608
  125.7 7.7 %slice-start.3 = ((s8[12582912]{0:T(1024)(128)(4,1)}), s8[4194304]{0:T(1024)(128)(4,1)S(1)}, s32[]{:S(2)}) async-start(s8[12582912]{0:T(1024)(128)(4,1)} %bitcast.61), calls=%async_computation.8 | async-start | bytes 8388608
  125.7 7.7 %slice-start.4 = ((s8[12582912]{0:T(1024)(128)(4,1)}), s8[4194304]{0:T(1024)(128)(4,1)S(1)}, s32[]{:S(2)}) async-start(s8[12582912]{0:T(1024)(128)(4,1)} %bitcast.61), calls=%async_computation.9 | async-start | bytes 8388608
  208.6 4.7 %copy-start.4 = (f32[128,2]{0,1:T(2,128)S(1)}, f32[128,2]{0,1:T(2,128)}, u32[]{:S(2)}) copy-start(f32[128,2]{0,1:T(2,128)} %param.17) | copy-start | bytes 3076
  208.6 42.6 %all-to-all-start.1 = ((bf16[8,32,3072]{2,1,0:T(8,128)(2,1)}), bf16[8,32,3072]{2,1,0:T(8,128)(2,1)S(1)}, u32[]{:S(2)}, u32[]{:S(2)}) async-start(bf16[8,32,3072]{2,1,0:T(8,128)(2,1)} %bitcast.53), calls=%async_computation.1 | async-start | bytes 3145728 | tf_op jit(solution)/shard_map/all_to_all | solution.py:161
Sparse Core Ops, SparseCore 0:
  10.2 26.6 all-gather.2
  39.1 22.5 all-gather.4
  138.1 60.5 all-reduce.2
where the time goes:
time: 261 us; the launch traced here: 260 us
  waiting for transfers between devices  134 us (51%)
  blocking collectives  46.7 us (18%)
  matrix products  41.9 us (16%)
  local copies, waits for them, and re-layouts  14 us (5%)
  between operations  14 us (5%)
  starting transfers between devices  4.86 us (2%)
  other arithmetic  4.82 us (2%)
    psum x1, waiting for transfers between devices, shards(): lax.psum(part_up.astype(jnp.bfloat16), 'tr').astype(jnp.float32)  60.7 us
    all_to_all x1, blocking collectives, shards(): lax.all_to_all(outgoing, ('ep', 'tc'), split_axis=0, concat_axis=0, tiled...  41.6 us
    all_to_all x1, waiting for transfers between devices, shards(): lax.all_to_all(down_part, ('ep', 'tc'), split_axis=0, concat_axis=0, tile...  36.6 us
    all_gather x1, waiting for transfers between devices, shards(): lax.all_gather(key_rows, ('ep', 'tc'), axis=0, tiled=True)  21.2 us
    all_gather x1, waiting for transfers between devices, shards(): lax.all_gather(value_rows, ('ep', 'tc'), axis=0, tiled=True)  15.5 us
    dot_general x1, matrix products, shards(): jnp.dot(hidden, w_down, preferred_element_type=jnp.float32)  10 us
    dot_general x2, matrix products, score_block(): jnp.einsum('hrk,khd->hrd', exponent.astype(jnp.bfloat16), value_heads, pr...  8.7 us
    dot_general x2, matrix products, score_block(): jnp.einsum('hrd,khd->hrk', query_heads, key_heads, preferred_element_type...  8.01 us
  transfers between devices with their start and end apart: 4, of which 4 were waited for; matrix products, arithmetic and copies ran while one was open for 7% of the time, Pallas kernels for 0%

commit v1 on v0

--- a/solution.py
+++ b/solution.py
@@ -3,6 +3,8 @@
 import jax
 import jax.numpy as jnp
 from jax import lax
+from jax.experimental import pallas as pl
+from jax.experimental.pallas import tpu as pltpu
 from jax.sharding import PartitionSpec as P
 
 D = 6144
@@ -170,6 +172,679 @@
     return (attention, expert_mix)
 
 
+col_tiles = 4
+row_slots = 32
+MESH = pl.DeviceIdType.MESH
+
+
+def layer_kernel(
+    query_ref,
+    key_ref,
+    value_ref,
+    residual_ref,
+    segment_ref,
+    route_ref,
+    weight_ref,
+    gain_ref,
+    gate_hbm,
+    up_hbm,
+    down_hbm,
+    attention_ref,
+    mix_ref,
+    gate_w,
+    up_w,
+    down_w,
+    context,
+    best,
+    total,
+    accumulated,
+    mixed,
+    sum_out,
+    sum_in,
+    slot_rows,
+    cross_rows,
+    parts,
+    parts_in,
+    hidden,
+    down,
+    down_in,
+    reduced,
+    outer_in,
+    returned,
+    load_sem,
+    ctx_send,
+    ctx_recv,
+    sum_send,
+    sum_recv,
+    row_send,
+    row_recv,
+    part_send,
+    part_recv,
+    hid_send,
+    hid_recv,
+    down_send,
+    down_recv,
+    outer_send,
+    outer_recv,
+    ret_send,
+    ret_recv,
+):
+    tokens, width = query_ref.shape
+    kv_width = key_ref.shape[1]
+    kv_count = kv_width // HD
+    group = QH // KVH
+    hidden_width = gate_w.shape[1]
+    tile_h = hidden_width // col_tiles
+    tile_f = width // col_tiles
+    half = 2 * row_slots
+    z = lax.axis_index("ep")
+    x = lax.axis_index("tr")
+    c = lax.axis_index("tc")
+    pair = z // 2
+    partner = z + 1 - 2 * lax.rem(z, 2)
+    other_inner = 2 - pair
+    other_outer = 3 - 3 * pair
+    my_inner = 1 + pair
+    my_outer = 3 * pair
+    is_inner = z == my_inner
+    sibling = {"tc": 1 - c}
+    across = {"tr": 1 - x}
+
+    loads = [
+        pltpu.make_async_copy(gate_hbm, gate_w, load_sem.at[0]),
+        pltpu.make_async_copy(up_hbm, up_w, load_sem.at[1]),
+        pltpu.make_async_copy(down_hbm, down_w, load_sem.at[2]),
+    ]
+    for load in loads:
+        load.start()
+
+    barrier = pltpu.get_barrier_semaphore()
+    for step in range(1, 4):
+        there = lax.rem(z + step, 4)
+        pl.semaphore_signal(barrier, inc=1, device_id={"ep": there}, device_id_type=MESH)
+    pl.semaphore_signal(barrier, inc=1, device_id=sibling, device_id_type=MESH)
+    pl.semaphore_signal(barrier, inc=1, device_id=across, device_id_type=MESH)
+
+    def send(src, dst, send_sem, recv_sem, target):
+        return pltpu.make_async_remote_copy(
+            src_ref=src,
+            dst_ref=dst,
+            send_sem=send_sem,
+            recv_sem=recv_sem,
+            device_id=target,
+            device_id_type=MESH,
+        )
+
+    own_ctx = pl.ds(pl.multiple_of(c * tokens, tokens), tokens)
+    sib_ctx = pl.ds(pl.multiple_of((1 - c) * tokens, tokens), tokens)
+    context[0, own_ctx, :kv_width] = key_ref[...]
+    context[0, own_ctx, kv_width:] = value_ref[...]
+    pl.semaphore_wait(barrier, 5)
+
+    def ctx_copy(from_slot, to_slot, number, recv, target):
+        return send(
+            context.at[from_slot, own_ctx],
+            context.at[to_slot, own_ctx],
+            ctx_send.at[number],
+            ctx_recv.at[recv],
+            target,
+        )
+
+    up_chip = {"ep": lax.rem(z + 1, 4)}
+    own_up = ctx_copy(0, 1, 0, 0, up_chip)
+    near_up = ctx_copy(1, 2, 1, 1, up_chip)
+    own_sib = ctx_copy(0, 0, 2, 2, sibling)
+    near_sib = ctx_copy(1, 1, 3, 3, sibling)
+    far_sib = ctx_copy(2, 2, 4, 4, sibling)
+
+    @pl.when(z < 3)
+    def _():
+        own_up.start()
+
+    own_sib.start()
+
+    lane = lax.broadcasted_iota(jnp.int32, (tokens, tokens), 1)
+    sub = lax.broadcasted_iota(jnp.int32, (tokens, tokens), 0)
+    upto = jnp.where(sub <= lane, 1.0, 0.0).astype(jnp.bfloat16)
+
+    def placement(expert):
+        first = jnp.broadcast_to(route_ref[0:1, :], (tokens, tokens)) == expert
+        second = jnp.broadcast_to(route_ref[1:2, :], (tokens, tokens)) == expert
+        weight = jnp.where(
+            first, jnp.broadcast_to(weight_ref[0:1, :], (tokens, tokens)), 0.0
+        ) + jnp.where(second, jnp.broadcast_to(weight_ref[1:2, :], (tokens, tokens)), 0.0)
+        named = jnp.where(first | second, 1.0, 0.0)
+        order = jnp.dot(named.astype(jnp.bfloat16), upto, preferred_element_type=jnp.float32)
+        wanted = (lax.rem(sub, row_slots) + 1).astype(jnp.float32)
+        place = jnp.where((order == wanted) & (named > 0.5), 1.0, 0.0)
+        return place, weight
+
+    own_place, own_weight = placement(pair)
+    cross_place, cross_weight = placement(1 - pair)
+
+    scale = 1.0 / math.sqrt(HD)
+    block = 2 * z + c
+    row_seg = jnp.transpose(
+        jnp.broadcast_to(segment_ref[pl.ds(block, 1), :].astype(jnp.float32), (tokens, tokens))
+    )
+    row_seg = jnp.concatenate([row_seg, row_seg], axis=1)
+
+    def attend(slot):
+        low = 2 * (z - slot)
+        key_seg = jnp.concatenate(
+            [segment_ref[pl.ds(low, 1), :], segment_ref[pl.ds(low + 1, 1), :]], axis=1
+        ).astype(jnp.float32)
+        visible = row_seg == jnp.broadcast_to(key_seg, (tokens, 2 * tokens))
+        if slot == 0:
+            key_pos = lax.broadcasted_iota(jnp.int32, (tokens, 2 * tokens), 1)
+            row_pos = c * tokens + lax.broadcasted_iota(jnp.int32, (tokens, 2 * tokens), 0)
+            visible = visible & (key_pos <= row_pos)
+        bias = jnp.where(visible, 0.0, masked_score)
+
+        def one_head(j, carry):
+            heads = [
+                query_ref[:, pl.ds(pl.multiple_of((j * group + g) * HD, HD), HD)]
+                for g in range(group)
+            ]
+            queries = jnp.concatenate(heads, axis=0)
+            keys = context[slot, :, pl.ds(pl.multiple_of(j * HD, HD), HD)]
+            values = context[slot, :, pl.ds(pl.multiple_of(kv_width + j * HD, HD), HD)]
+            scores = lax.dot_general(
+                queries, keys, (((1,), (1,)), ((), ())), preferred_element_type=jnp.float32
+            )
+            scores = (scores * scale).reshape(group, tokens, 2 * tokens)
+            scores = jnp.where((bias < -1.0)[None], masked_score, scores)
+            scores = scores.reshape(group * tokens, 2 * tokens)
+            peak = jnp.max(scores, axis=1, keepdims=True)
+            if slot > 0:
+                old = best[j][:, :1]
+                peak = jnp.maximum(peak, old)
+            exponent = jnp.exp(scores - peak)
+            amount = jnp.sum(exponent, axis=1, keepdims=True)
+            product = jnp.dot(
+                exponent.astype(jnp.bfloat16), values, preferred_element_type=jnp.float32
+            )
+            if slot > 0:
+                factor = jnp.exp(old - peak)
+                amount = amount + total[j][:, :1] * factor
+                product = product + accumulated[j] * factor
+            best[j] = jnp.broadcast_to(peak, (group * tokens, HD))
+            total[j] = jnp.broadcast_to(amount, (group * tokens, HD))
+            accumulated[j] = product
+            return carry
+
+        lax.fori_loop(0, kv_count, one_head, 0)
+
+    own_sib.wait_recv()
+    attend(0)
+
+    @pl.when(z >= 1)
+    def _():
+        own_up.wait_recv()
+
+        @pl.when(z < 3)
+        def _():
+            near_up.start()
+
+        near_sib.start()
+        near_sib.wait_recv()
+        attend(1)
+
+    @pl.when(z >= 2)
+    def _():
+        near_up.wait_recv()
+        far_sib.start()
+        far_sib.wait_recv()
+        attend(2)
+
+    squares = jnp.zeros((tokens, HD), jnp.float32)
+
+    def finish_head(j, squares):
+        for g in range(group):
+            rows = slice(g * tokens, (g + 1) * tokens)
+            cols = pl.ds(pl.multiple_of((j * group + g) * HD, HD), HD)
+            result = (accumulated[j, rows, :] / total[j, rows, :]).astype(jnp.bfloat16)
+            attention_ref[:, cols] = result
+            both = (
+                residual_ref[:, cols].astype(jnp.float32) + result.astype(jnp.float32)
+            ).astype(jnp.bfloat16)
+            mixed[:, cols] = both
+            wide = both.astype(jnp.float32)
+            squares = squares + wide * wide
+        return squares
+
+    squares = lax.fori_loop(0, kv_count, finish_head, squares)
+    my_sum = jnp.broadcast_to(jnp.sum(jnp.transpose(squares), axis=0, keepdims=True), (8, tokens))
+    sum_out[...] = my_sum
+    sum_copy = send(sum_out, sum_in, sum_send, sum_recv, across)
+    sum_copy.start()
+    sum_copy.wait_recv()
+    both_sums = jnp.broadcast_to((my_sum + sum_in[...])[0:1, :], (tokens, tokens))
+    inv_rms = jnp.transpose(lax.rsqrt(both_sums / D + 1e-05))[:, :1]
+    picks = jnp.concatenate([own_place[:row_slots], cross_place[:row_slots]], axis=0).astype(
+        jnp.bfloat16
+    )
+    own_near = pl.ds(pl.multiple_of(c * half, row_slots), row_slots)
+    own_far = pl.ds(pl.multiple_of(c * half + row_slots, row_slots), row_slots)
+
+    def pack(m, carry):
+        cols = pl.ds(pl.multiple_of(m * tile_f, tile_f), tile_f)
+        normed = (mixed[:, cols].astype(jnp.float32) * inv_rms * gain_ref[:, cols]).astype(
+            jnp.bfloat16
+        )
+        packed = jnp.dot(picks, normed, preferred_element_type=jnp.float32).astype(jnp.bfloat16)
+        slot_rows[0, own_near, cols] = packed[:row_slots]
+        cross_rows[:, cols] = packed[row_slots:]
+        return carry
+
+    lax.fori_loop(0, col_tiles, pack, 0)
+
+    def row_copy(chunk, place, number, recv, target):
+        return send(
+            slot_rows.at[chunk, place],
+            slot_rows.at[chunk, place],
+            row_send.at[number],
+            row_recv.at[recv],
+            target,
+        )
+
+    to_partner = send(
+        slot_rows.at[0, own_near],
+        slot_rows.at[0, own_far],
+        row_send.at[0],
+        row_recv.at[0],
+        {"ep": partner},
+    )
+    cross_target = {"ep": other_inner}
+    from_inner = send(
+        cross_rows, slot_rows.at[1, own_near], row_send.at[1], row_recv.at[1], cross_target
+    )
+    from_outer = send(
+        cross_rows, slot_rows.at[1, own_far], row_send.at[1], row_recv.at[2], cross_target
+    )
+    own_share = row_copy(0, own_near, 2, 3, sibling)
+    partner_share = row_copy(0, own_far, 3, 4, sibling)
+    inner_share = row_copy(1, own_near, 4, 5, sibling)
+    outer_share = row_copy(1, own_far, 5, 6, sibling)
+    pass_inner = row_copy(1, own_near, 6, 1, {"ep": my_outer})
+    pass_outer = row_copy(1, own_far, 7, 2, {"ep": my_outer})
+
+    to_partner.start()
+
+    @pl.when(is_inner)
+    def _():
+        from_inner.start()
+
+    @pl.when(jnp.logical_not(is_inner))
+    def _():
+        from_outer.start()
+
+    own_share.start()
+
+    def part_copy(chunk, n):
+        number = chunk * col_tiles + n
+        rows = pl.ds(pl.multiple_of((1 - x) * half, half), half)
+        return send(
+            parts.at[number, rows],
+            parts_in.at[number],
+            part_send.at[number],
+            part_recv.at[number],
+            across,
+        )
+
+    def hidden_copy(chunk, n):
+        number = chunk * col_tiles + n
+        rows = pl.ds(pl.multiple_of(x * half, half), half)
+        return send(
+            hidden.at[number, rows],
+            hidden.at[number, rows],
+            hid_send.at[number],
+            hid_recv.at[number],
+            across,
+        )
+
+    def gate_up(chunk):
+        def one_tile(n, carry):
+            cols = pl.ds(pl.multiple_of(n * tile_h, tile_h), tile_h)
+            number = chunk * col_tiles + n
+            parts[number, :, :tile_h] = jnp.dot(
+                slot_rows[chunk], gate_w[:, cols], preferred_element_type=jnp.float32
+            ).astype(jnp.bfloat16)
+            parts[number, :, tile_h:] = jnp.dot(
+                slot_rows[chunk], up_w[:, cols], preferred_element_type=jnp.float32
+            ).astype(jnp.bfloat16)
+            part_copy(chunk, n).start()
+            return carry
+
+        lax.fori_loop(0, col_tiles, one_tile, 0)
+
+    def activate(chunk):
+        def one_tile(n, carry):
+            number = chunk * col_tiles + n
+            part_copy(chunk, n).wait_recv()
+            rows = pl.ds(pl.multiple_of(x * half, half), half)
+            sums = parts[number, rows, :].astype(jnp.float32) + parts_in[number].astype(
+                jnp.float32
+            )
+            gate = sums[:, :tile_h]
+            hidden[number, rows, :] = (
+                gate / (1.0 + jnp.exp(-gate)) * sums[:, tile_h:]
+            ).astype(jnp.bfloat16)
+            hidden_copy(chunk, n).start()
+            return carry
+
+        lax.fori_loop(0, col_tiles, one_tile, 0)
+
+    def await_hidden(chunk):
+        def one_tile(n, carry):
+            hidden_copy(chunk, n).wait_recv()
+            return carry
+
+        lax.fori_loop(0, col_tiles, one_tile, 0)
+
+    def down_copy(chunk, m):
+        number = chunk * col_tiles + m
+        rows = pl.ds(pl.multiple_of((1 - c) * half, half), half)
+        return send(
+            down.at[number, rows],
+            down_in.at[number],
+            down_send.at[number],
+            down_recv.at[number],
+            sibling,
+        )
+
+    def project(chunk):
+        def one_tile(m, carry):
+            cols = pl.ds(pl.multiple_of(m * tile_f, tile_f), tile_f)
+            number = chunk * col_tiles + m
+            units = jnp.concatenate(
+                [hidden[chunk * col_tiles + n] for n in range(col_tiles)], axis=1
+            )
+            down[number] = jnp.dot(
+                units, down_w[:, cols], preferred_element_type=jnp.float32
+            ).astype(jnp.bfloat16)
+            down_copy(chunk, m).start()
+            return carry
+
+        lax.fori_loop(0, col_tiles, one_tile, 0)
+
+    def chip_sum(chunk, m):
+        number = chunk * col_tiles + m
+        down_copy(chunk, m).wait_recv()
+        rows = pl.ds(pl.multiple_of(c * half, half), half)
+        return down[number, rows, :].astype(jnp.float32) + down_in[number].astype(jnp.float32)
+
+    near_rows = pl.ds(0, row_slots)
+    far_rows = pl.ds(row_slots, row_slots)
+    cross_back = pl.ds(half, row_slots)
+
+    def partner_back(m):
+        return send(
+            reduced.at[m, far_rows],
+            returned.at[m, far_rows],
+            ret_send.at[m],
+            ret_recv.at[m],
+            {"ep": partner},
+        )
+
+    def outer_copy(m):
+        return send(
+            reduced.at[col_tiles + m],
+            outer_in.at[m],
+            outer_send.at[m],
+            outer_recv.at[m],
+            {"ep": my_inner},
+        )
+
+    def inner_back(m):
+        return send(
+            reduced.at[col_tiles + m, near_rows],
+            returned.at[m, cross_back],
+            ret_send.at[col_tiles + m],
+            ret_recv.at[col_tiles + m],
+            {"ep": other_inner},
+        )
+
+    def outer_back(m):
+        return send(
+            reduced.at[col_tiles + m, far_rows],
+            returned.at[m, cross_back],
+            ret_send.at[2 * col_tiles + m],
+            ret_recv.at[col_tiles + m],
+            {"ep": other_outer},
+        )
+
+    to_partner.wait_recv()
+    partner_share.start()
+    own_share.wait_recv()
+    partner_share.wait_recv()
+    loads[0].wait()
+    loads[1].wait()
+    gate_up(0)
+
+    from_inner.wait_recv()
+    inner_share.start()
+
+    @pl.when(is_inner)
+    def _():
+        pass_inner.start()
+
+    from_outer.wait_recv()
+    outer_share.start()
+
+    @pl.when(is_inner)
+    def _():
+        pass_outer.start()
+
+    activate(0)
+    inner_share.wait_recv()
+    outer_share.wait_recv()
+    gate_up(1)
+    loads[2].wait()
+    await_hidden(0)
+    project(0)
+
+    def return_own(m, carry):
+        sums = chip_sum(0, m).astype(jnp.bfloat16)
+        returned[m, near_rows, :] = sums[:row_slots]
+        reduced[m] = sums
+        partner_back(m).start()
+        return carry
+
+    lax.fori_loop(0, col_tiles, return_own, 0)
+
+    activate(1)
+    await_hidden(1)
+    project(1)
+
+    @pl.when(jnp.logical_not(is_inner))
+    def _():
+        def hand_over(m, carry):
+            reduced[col_tiles + m] = chip_sum(1, m).astype(jnp.bfloat16)
+            outer_copy(m).start()
+            return carry
+
+        lax.fori_loop(0, col_tiles, hand_over, 0)
+
+    @pl.when(is_inner)
+    def _():
+        def hand_back(m, carry):
+            sums = chip_sum(1, m)
+            outer_copy(m).wait_recv()
+            reduced[col_tiles + m] = (sums + outer_in[m].astype(jnp.float32)).astype(jnp.bfloat16)
+            outer_back(m).start()
+            inner_back(m).start()
+            return carry
+
+        lax.fori_loop(0, col_tiles, hand_back, 0)
+
+    own_spread = jnp.transpose(own_place)[:, :half].astype(jnp.bfloat16)
+    cross_spread = jnp.transpose(cross_place)[:, :row_slots].astype(jnp.bfloat16)
+    own_scale = jnp.transpose(own_weight)[:, :1]
+    cross_scale = jnp.transpose(cross_weight)[:, :1]
+
+    def combine(m, carry):
+        cols = pl.ds(pl.multiple_of(m * tile_f, tile_f), tile_f)
+        partner_back(m).wait_recv()
+        own_part = jnp.dot(own_spread, returned[m, :half, :], preferred_element_type=jnp.float32)
+        inner_back(m).wait_recv()
+        cross_part = jnp.dot(
+            cross_spread, returned[m, half:, :], preferred_element_type=jnp.float32
+        )
+        mix_ref[:, cols] = (own_scale * own_part + cross_scale * cross_part).astype(jnp.bfloat16)
+        return carry
+
+    lax.fori_loop(0, col_tiles, combine, 0)
+
+    @pl.when(z < 3)
+    def _():
+        own_up.wait_send()
+
+    @pl.when((z >= 1) & (z < 3))
+    def _():
+        near_up.wait_send()
+
+    own_sib.wait_send()
+
+    @pl.when(z >= 1)
+    def _():
+        near_sib.wait_send()
+
+    @pl.when(z >= 2)
+    def _():
+        far_sib.wait_send()
+
+    sum_copy.wait_send()
+    for copy in (to_partner, from_inner, own_share, partner_share, inner_share, outer_share):
+        copy.wait_send()
+
+    @pl.when(is_inner)
+    def _():
+        pass_inner.wait_send()
+        pass_outer.wait_send()
+
+    def drain(n, carry):
+        for chunk in range(2):
+            part_copy(chunk, n).wait_send()
+            hidden_copy(chunk, n).wait_send()
+            down_copy(chunk, n).wait_send()
+        partner_back(n).wait_send()
+        return carry
+
+    lax.fori_loop(0, col_tiles, drain, 0)
+
+    @pl.when(is_inner)
+    def _():
+        def drain_inner(m, carry):
+            inner_back(m).wait_send()
+            outer_back(m).wait_send()
+            return carry
+
+        lax.fori_loop(0, col_tiles, drain_inner, 0)
+
+    @pl.when(jnp.logical_not(is_inner))
+    def _():
+        def drain_outer(m, carry):
+            outer_copy(m).wait_send()
+            return carry
+
+        lax.fori_loop(0, col_tiles, drain_outer, 0)
+
+
+def fused_shards(
+    residual,
+    query_rows,
+    key_rows,
+    value_rows,
+    segments,
+    routes,
+    gate_weights,
+    norm_gain,
+    w_gate,
+    w_up,
+    w_down,
+):
+    tokens, width = residual.shape
+    kv_width = key_rows.shape[1]
+    kv_count = kv_width // HD
+    group_rows = tokens * (QH // KVH)
+    hidden_width = w_gate.shape[1]
+    tile_h = hidden_width // col_tiles
+    tile_f = width // col_tiles
+    half = 2 * row_slots
+    low = jnp.bfloat16
+    vmem = pl.BlockSpec(memory_space=pltpu.VMEM)
+    hbm = pl.BlockSpec(memory_space=pl.ANY)
+    dma = pltpu.SemaphoreType.DMA
+    return pl.pallas_call(
+        layer_kernel,
+        out_shape=(
+            jax.ShapeDtypeStruct((tokens, width), low),
+            jax.ShapeDtypeStruct((tokens, width), low),
+        ),
+        in_specs=[vmem] * 8 + [hbm] * 3,
+        out_specs=(vmem, vmem),
+        scratch_shapes=[
+            pltpu.VMEM(w_gate.shape, low),
+            pltpu.VMEM(w_up.shape, low),
+            pltpu.VMEM(w_down.shape, low),
+            pltpu.VMEM((3, 2 * tokens, 2 * kv_width), low),
+            pltpu.VMEM((kv_count, group_rows, HD), jnp.float32),
+            pltpu.VMEM((kv_count, group_rows, HD), jnp.float32),
+            pltpu.VMEM((kv_count, group_rows, HD), jnp.float32),
+            pltpu.VMEM((tokens, width), low),
+            pltpu.VMEM((8, tokens), jnp.float32),
+            pltpu.VMEM((8, tokens), jnp.float32),
+            pltpu.VMEM((2, 2 * half, width), low),
+            pltpu.VMEM((row_slots, width), low),
+            pltpu.VMEM((2 * col_tiles, 2 * half, 2 * tile_h), low),
+            pltpu.VMEM((2 * col_tiles, half, 2 * tile_h), low),
+            pltpu.VMEM((2 * col_tiles, 2 * half, tile_h), low),
+            pltpu.VMEM((2 * col_tiles, 2 * half, tile_f), low),
+            pltpu.VMEM((2 * col_tiles, half, tile_f), low),
+            pltpu.VMEM((2 * col_tiles, half, tile_f), low),
+            pltpu.VMEM((col_tiles, half, tile_f), low),
+            pltpu.VMEM((col_tiles, half + row_slots, tile_f), low),
+            dma((3,)),
+            dma((5,)),
+            dma((5,)),
+            dma,
+            dma,
+            dma((8,)),
+            dma((7,)),
+            dma((2 * col_tiles,)),
+            dma((2 * col_tiles,)),
+            dma((2 * col_tiles,)),
+            dma((2 * col_tiles,)),
+            dma((2 * col_tiles,)),
+            dma((2 * col_tiles,)),
+            dma((col_tiles,)),
+            dma((col_tiles,)),
+            dma((3 * col_tiles,)),
+            dma((2 * col_tiles,)),
+        ],
+        compiler_params=pltpu.CompilerParams(
+            collective_id=0, has_side_effects=True, vmem_limit_bytes=63 * 1024 * 1024
+        ),
+        cost_estimate=pl.CostEstimate(
+            flops=10_000_000_000, bytes_accessed=40_000_000, transcendentals=3_000_000
+        ),
+        name="layer",
+    )(
+        query_rows,
+        key_rows,
+        value_rows,
+        residual,
+        segments.reshape(-1, tokens),
+        routes.T,
+        gate_weights.T,
+        norm_gain.reshape(1, width),
+        w_gate,
+        w_up,
+        w_down,
+    )
+
+
 def solution(mesh):
     in_specs = (
         P(("rep", "ep", "tc"), "tr"),
@@ -185,4 +860,6 @@
         P(("ep", "tc"), "tr"),
     )
     out_specs = (P(("rep", "ep", "tc"), "tr"), P(("rep", "ep", "tc"), "tr"))
-    return jax.shard_map(shards, mesh=mesh, in_specs=in_specs, out_specs=out_specs, check_vma=False)
+    fits = (mesh.shape["ep"], mesh.shape["tr"], mesh.shape["tc"]) == (4, 2, 2)
+    body = fused_shards if fits else shards
+    return jax.shard_map(body, mesh=mesh, in_specs=in_specs, out_specs=out_specs, check_vma=False)

time: 261 us -> 109 us (0.42)
  waiting for transfers between devices: 134 us -> 0 us
  Pallas kernels: 0 us -> 104 us
  blocking collectives: 46.7 us -> 0 us
  matrix products: 41.9 us -> 0 us
  between operations: 14 us -> 0.64 us
  local copies, waits for them, and re-layouts: 14 us -> 4.13 us
  starting transfers between devices: 4.86 us -> 0 us
  other arithmetic: 4.82 us -> 0 us
    pallas_call x0 -> x1, Pallas kernels: none -> 104 us  [fused_shards(): pl.pallas_call(layer_kernel, out_shape=(jax.ShapeDtypeStruct((tokens, wid...]
    psum x1 -> x0, waiting for transfers between devices: 60.7 us -> none  [shards(): lax.psum(part_up.astype(jnp.bfloat16), 'tr').astype(jnp.float32)]
    dot_general x9 -> x0, matrix products: 41.9 us -> none  [the longest x1 10 us: shards(): jnp.dot(hidden, w_down, preferred_element_type=jnp.float32)]
    all_to_all x1 -> x0, blocking collectives: 41.6 us -> none  [shards(): lax.all_to_all(outgoing, ('ep', 'tc'), split_axis=0, concat_axis=0, tiled...]
    all_gather x2 -> x0, waiting for transfers between devices: 36.7 us -> none  [the longest x1 21.2 us: shards(): lax.all_gather(key_rows, ('ep', 'tc'), axis=0, tiled=True)]
    all_to_all x1 -> x0, waiting for transfers between devices: 36.6 us -> none  [shards(): lax.all_to_all(down_part, ('ep', 'tc'), split_axis=0, concat_axis=0, tile...]
    psum x1 -> x0, blocking collectives: 5.11 us -> none  [shards(): squares = lax.psum(jnp.sum(mixed_wide * mixed_wide, axis=1), 'tr')]
    all_to_all x1 -> x0, starting transfers between devices: 4.74 us -> none  [shards(): lax.all_to_all(down_part, ('ep', 'tc'), split_axis=0, concat_axis=0, tile...]
  transfers between devices with their start and end apart: 4 -> 0, of which waited for: 4 -> 0; matrix products, arithmetic and copies ran while one was open for 7% -> 0% of each run, Pallas kernels for 0% -> 0%
where the time goes in v1:
time: 109 us
  Pallas kernels  104 us (95%)
  local copies, waits for them, and re-layouts  4.13 us (4%)
    pallas_call x1, Pallas kernels, fused_shards(): pl.pallas_call(layer_kernel, out_shape=(jax.ShapeDtypeStruct((tokens, wid...  104 us
    unnamed x2, local copies, waits for them, and re-layouts  4.13 us

profile of v1, /device:TPU:0, one launch (start us, length us, event | category | flops | bytes accessed | tf_op | source)
XLA Modules:
  0.0 108.8 jit_solution(9873067476084347255)
XLA Ops:
  0.6 104.0 %layer.1 = (bf16[128,3072]{1,0:T(8,128)(2,1)}, bf16[128,3072]{1,0:T(8,128)(2,1)}) custom-call(bf16[128,3072]{1,0:T(8,128)(2,1)} %query_ref.1, bf16[128,512]{1,0:T(8,128)(2,1)} %key_ref.1, bf16[128,512]{1,0:T(8,128)(2,1)} %value_ref.1, bf16[128,3072]{1,0:T(8,128)(2,1)} %residual_ref.1, s32[8,128]{1,0:T(8,128)} %bitcast.5, s32[2,128]{1,0:T(2,128)} %bitcast.6, ...), custom_call_target="tpu_custom_call" | custom-call | flops 10000000000 | bytes 40000000 | tf_op jit(solution)/shard_map/layer/pallas_call | solution.py:779
  104.6 2.1 %copy.15 = bf16[128,3072]{1,0:T(8,128)(2,1)} copy(bf16[128,3072]{1,0:T(8,128)(2,1)} %get-tuple-element.4) | data formatting | bytes 1572864
  106.7 2.1 %copy.16 = bf16[128,3072]{1,0:T(8,128)(2,1)} copy(bf16[128,3072]{1,0:T(8,128)(2,1)} %get-tuple-element.5) | data formatting | bytes 1572864

commit v2 on v1

--- a/solution.py
+++ b/solution.py
@@ -189,8 +189,7 @@
     gate_hbm,
     up_hbm,
     down_hbm,
-    attention_ref,
-    mix_ref,
+    both_ref,
     gate_w,
     up_w,
     down_w,
@@ -375,6 +374,55 @@
 
         lax.fori_loop(0, kv_count, one_head, 0)
 
+    own_near = pl.ds(pl.multiple_of(c * half, row_slots), row_slots)
+    own_far = pl.ds(pl.multiple_of(c * half + row_slots, row_slots), row_slots)
+
+    def row_copy(chunk, place, number, recv, target):
+        return send(
+            slot_rows.at[chunk, place],
+            slot_rows.at[chunk, place],
+            row_send.at[number],
+            row_recv.at[recv],
+            target,
+        )
+
+    to_partner = send(
+        slot_rows.at[0, own_near],
+        slot_rows.at[0, own_far],
+        row_send.at[0],
+        row_recv.at[0],
+        {"ep": partner},
+    )
+    cross_target = {"ep": other_inner}
+    from_inner = send(
+        cross_rows, slot_rows.at[1, own_near], row_send.at[1], row_recv.at[1], cross_target
+    )
+    from_outer = send(
+        cross_rows, slot_rows.at[1, own_far], row_send.at[1], row_recv.at[2], cross_target
+    )
+    own_share = row_copy(0, own_near, 2, 3, sibling)
+    partner_share = row_copy(0, own_far, 3, 4, sibling)
+    inner_share = row_copy(1, own_near, 4, 5, sibling)
+    outer_share = row_copy(1, own_far, 5, 6, sibling)
+    pass_inner = row_copy(1, own_near, 6, 1, {"ep": my_outer})
+    pass_outer = row_copy(1, own_far, 7, 2, {"ep": my_outer})
+
+    def relay_cross():
+        from_inner.wait_recv()
+
+        @pl.when(is_inner)
+        def _():
+            pass_inner.start()
+
+        inner_share.start()
+        from_outer.wait_recv()
+
+        @pl.when(is_inner)
+        def _():
+            pass_outer.start()
+
+        outer_share.start()
+
     own_sib.wait_recv()
     attend(0)
 
@@ -396,6 +444,10 @@
         far_sib.start()
         far_sib.wait_recv()
         attend(2)
+
+    @pl.when(z == 2)
+    def _():
+        relay_cross()
 
     squares = jnp.zeros((tokens, HD), jnp.float32)
 
@@ -404,7 +456,7 @@
             rows = slice(g * tokens, (g + 1) * tokens)
             cols = pl.ds(pl.multiple_of((j * group + g) * HD, HD), HD)
             result = (accumulated[j, rows, :] / total[j, rows, :]).astype(jnp.bfloat16)
-            attention_ref[:, cols] = result
+            both_ref[0, :, cols] = result
             both = (
                 residual_ref[:, cols].astype(jnp.float32) + result.astype(jnp.float32)
             ).astype(jnp.bfloat16)
@@ -424,9 +476,6 @@
     picks = jnp.concatenate([own_place[:row_slots], cross_place[:row_slots]], axis=0).astype(
         jnp.bfloat16
     )
-    own_near = pl.ds(pl.multiple_of(c * half, row_slots), row_slots)
-    own_far = pl.ds(pl.multiple_of(c * half + row_slots, row_slots), row_slots)
-
     def pack(m, carry):
         cols = pl.ds(pl.multiple_of(m * tile_f, tile_f), tile_f)
         normed = (mixed[:, cols].astype(jnp.float32) * inv_rms * gain_ref[:, cols]).astype(
@@ -439,46 +488,15 @@
 
     lax.fori_loop(0, col_tiles, pack, 0)
 
-    def row_copy(chunk, place, number, recv, target):
-        return send(
-            slot_rows.at[chunk, place],
-            slot_rows.at[chunk, place],
-            row_send.at[number],
-            row_recv.at[recv],
-            target,
-        )
-
-    to_partner = send(
-        slot_rows.at[0, own_near],
-        slot_rows.at[0, own_far],
-        row_send.at[0],
-        row_recv.at[0],
-        {"ep": partner},
-    )
-    cross_target = {"ep": other_inner}
-    from_inner = send(
-        cross_rows, slot_rows.at[1, own_near], row_send.at[1], row_recv.at[1], cross_target
-    )
-    from_outer = send(
-        cross_rows, slot_rows.at[1, own_far], row_send.at[1], row_recv.at[2], cross_target
-    )
-    own_share = row_copy(0, own_near, 2, 3, sibling)
-    partner_share = row_copy(0, own_far, 3, 4, sibling)
-    inner_share = row_copy(1, own_near, 4, 5, sibling)
-    outer_share = row_copy(1, own_far, 5, 6, sibling)
-    pass_inner = row_copy(1, own_near, 6, 1, {"ep": my_outer})
-    pass_outer = row_copy(1, own_far, 7, 2, {"ep": my_outer})
+    @pl.when(is_inner)
+    def _():
+        from_inner.start()
+
+    @pl.when(jnp.logical_not(is_inner))
+    def _():
+        from_outer.start()
 
     to_partner.start()
-
-    @pl.when(is_inner)
-    def _():
-        from_inner.start()
-
-    @pl.when(jnp.logical_not(is_inner))
-    def _():
-        from_outer.start()
-
     own_share.start()
 
     def part_copy(chunk, n):
@@ -614,69 +632,88 @@
             {"ep": other_outer},
         )
 
-    to_partner.wait_recv()
-    partner_share.start()
-    own_share.wait_recv()
-    partner_share.wait_recv()
+    def take_own():
+        to_partner.wait_recv()
+        partner_share.start()
+        own_share.wait_recv()
+        partner_share.wait_recv()
+
+    def take_cross():
+        @pl.when(z != 2)
+        def _():
+            relay_cross()
+
+        inner_share.wait_recv()
+        outer_share.wait_recv()
+
+    def take(lower_first):
+        @pl.when(pair == lower_first)
+        def _():
+            take_own()
+
+        @pl.when(pair != lower_first)
+        def _():
+            take_cross()
+
+    def return_own():
+        def one_tile(m, carry):
+            sums = chip_sum(0, m).astype(jnp.bfloat16)
+            returned[m, near_rows, :] = sums[:row_slots]
+            reduced[m] = sums
+            partner_back(m).start()
+            return carry
+
+        lax.fori_loop(0, col_tiles, one_tile, 0)
+
+    def return_cross():
+        @pl.when(jnp.logical_not(is_inner))
+        def _():
+            def hand_over(m, carry):
+                reduced[col_tiles + m] = chip_sum(1, m).astype(jnp.bfloat16)
+                outer_copy(m).start()
+                return carry
+
+            lax.fori_loop(0, col_tiles, hand_over, 0)
+
+        @pl.when(is_inner)
+        def _():
+            def hand_back(m, carry):
+                sums = chip_sum(1, m)
+                outer_copy(m).wait_recv()
+                reduced[col_tiles + m] = (sums + outer_in[m].astype(jnp.float32)).astype(
+                    jnp.bfloat16
+                )
+                outer_back(m).start()
+                inner_back(m).start()
+                return carry
+
+            lax.fori_loop(0, col_tiles, hand_back, 0)
+
+    def give_back(lower_first):
+        @pl.when(pair == lower_first)
+        def _():
+            return_own()
+
+        @pl.when(pair != lower_first)
+        def _():
+            return_cross()
+
+    first, second = pair, 1 - pair
+    take(0)
     loads[0].wait()
     loads[1].wait()
-    gate_up(0)
-
-    from_inner.wait_recv()
-    inner_share.start()
-
-    @pl.when(is_inner)
-    def _():
-        pass_inner.start()
-
-    from_outer.wait_recv()
-    outer_share.start()
-
-    @pl.when(is_inner)
-    def _():
-        pass_outer.start()
-
-    activate(0)
-    inner_share.wait_recv()
-    outer_share.wait_recv()
-    gate_up(1)
+    gate_up(first)
+    activate(first)
+    take(1)
+    gate_up(second)
     loads[2].wait()
-    await_hidden(0)
-    project(0)
-
-    def return_own(m, carry):
-        sums = chip_sum(0, m).astype(jnp.bfloat16)
-        returned[m, near_rows, :] = sums[:row_slots]
-        reduced[m] = sums
-        partner_back(m).start()
-        return carry
-
-    lax.fori_loop(0, col_tiles, return_own, 0)
-
-    activate(1)
-    await_hidden(1)
-    project(1)
-
-    @pl.when(jnp.logical_not(is_inner))
-    def _():
-        def hand_over(m, carry):
-            reduced[col_tiles + m] = chip_sum(1, m).astype(jnp.bfloat16)
-            outer_copy(m).start()
-            return carry
-
-        lax.fori_loop(0, col_tiles, hand_over, 0)
-
-    @pl.when(is_inner)
-    def _():
-        def hand_back(m, carry):
-            sums = chip_sum(1, m)
-            outer_copy(m).wait_recv()
-            reduced[col_tiles + m] = (sums + outer_in[m].astype(jnp.float32)).astype(jnp.bfloat16)
-            outer_back(m).start()
-            inner_back(m).start()
-            return carry
-
-        lax.fori_loop(0, col_tiles, hand_back, 0)
+    await_hidden(first)
+    project(first)
+    give_back(0)
+    activate(second)
+    await_hidden(second)
+    project(second)
+    give_back(1)
 
     own_spread = jnp.transpose(own_place)[:, :half].astype(jnp.bfloat16)
     cross_spread = jnp.transpose(cross_place)[:, :row_slots].astype(jnp.bfloat16)
@@ -691,7 +728,7 @@
         cross_part = jnp.dot(
             cross_spread, returned[m, half:, :], preferred_element_type=jnp.float32
         )
-        mix_ref[:, cols] = (own_scale * own_part + cross_scale * cross_part).astype(jnp.bfloat16)
+        both_ref[1, :, cols] = (own_scale * own_part + cross_scale * cross_part).astype(jnp.bfloat16)
         return carry
 
     lax.fori_loop(0, col_tiles, combine, 0)
@@ -776,14 +813,11 @@
     vmem = pl.BlockSpec(memory_space=pltpu.VMEM)
     hbm = pl.BlockSpec(memory_space=pl.ANY)
     dma = pltpu.SemaphoreType.DMA
-    return pl.pallas_call(
+    both = pl.pallas_call(
         layer_kernel,
-        out_shape=(
-            jax.ShapeDtypeStruct((tokens, width), low),
-            jax.ShapeDtypeStruct((tokens, width), low),
-        ),
+        out_shape=jax.ShapeDtypeStruct((2, tokens, width), low),
         in_specs=[vmem] * 8 + [hbm] * 3,
-        out_specs=(vmem, vmem),
+        out_specs=vmem,
         scratch_shapes=[
             pltpu.VMEM(w_gate.shape, low),
             pltpu.VMEM(w_up.shape, low),
@@ -843,6 +877,7 @@
         w_up,
         w_down,
     )
+    return both[0], both[1]
 
 
 def solution(mesh):

time: 109 us -> 100 us (0.917)
  the two profiles are of different devices: /device:TPU:0 before, /device:TPU:24 now
where the time goes in v2:
time: 100 us
  Pallas kernels  97 us (97%)
  local copies, waits for them, and re-layouts  2.61 us (3%)
    pallas_call x1, Pallas kernels, fused_shards(): pl.pallas_call(layer_kernel, out_shape=jax.ShapeDtypeStruct((2, tokens, w...  97 us
    squeeze x1, local copies, waits for them, and re-layouts, fused_shards(): return (both[0], both[1])  2.61 us

profile of v2, /device:TPU:24, one launch (start us, length us, event | category | flops | bytes accessed | tf_op | source)
XLA Modules:
  0.0 100.3 jit_solution(3490751337026194957)
XLA Ops:
  0.6 97.0 %layer.1 = bf16[2,128,3072]{2,1,0:T(8,128)(2,1)} custom-call(bf16[128,3072]{1,0:T(8,128)(2,1)} %query_ref.1, bf16[128,512]{1,0:T(8,128)(2,1)} %key_ref.1, bf16[128,512]{1,0:T(8,128)(2,1)} %value_ref.1, bf16[128,3072]{1,0:T(8,128)(2,1)} %residual_ref.1, s32[8,128]{1,0:T(8,128)} %bitcast.9, s32[2,128]{1,0:T(2,128)} %bitcast.10, f32[2,128]{1,0:T(2,128)} %bitcast.11, ...), custom_call_target="tpu_custom_call" | custom-call | flops 10000000000 | bytes 40000000 | tf_op jit(solution)/shard_map/layer/pallas_call | solution.py:816
  97.7 2.6 %slice_bitcast_fusion = (bf16[128,3072]{1,0:T(8,128)(2,1)}, bf16[128,3072]{1,0:T(8,128)(2,1)}) fusion(bf16[2,128,3072]{2,1,0:T(8,128)(2,1)} %layer.1), kind=kLoop, calls=%fused_computation | loop fusion | bytes 3145728 | tf_op jit(solution)/shard_map/squeeze | solution.py:880
